TPU v7x, 512 devices: a whole 4x4x16 slice. The times are simulated.
512 devices in a mesh: section: 16 (over x, y), expert: 32 (over z, core).
Axes of the slice: x: 4, y: 4, z: 16, core: 2. Of those that a mesh axis runs over, the one named last changes fastest.
Arguments:
- stream: bfloat16 [16, 4096, 2560], P('section', 'expert'), may hold values from -6 to 6
- lengths: int32 [16, 16], P('section'), may hold values from 64 to 256, as said below
- routes: int32 [2, 16, 4096, 2], P(None, 'section', 'expert'), may hold values from 0 to 63, as said below
- norm_gains: bfloat16 [16, 2560], P('section'), may hold values from 0.099609375 to 1.8984375
- router_weights: bfloat16 [16, 2560, 64], P('section'), may hold values from -0.125 to 0.125
- up_weights: bfloat16 [16, 2560, 10240], P('section', None, 'expert'), may hold values from -0.125 to 0.125
- down_weights: bfloat16 [16, 10240, 2560], P('section', 'expert'), may hold values from -0.0625 to 0.0625
Outputs:
- advanced: bfloat16 [16, 4096, 2560], P('section', 'expert')
Inputs may be any that keep to these rules, and one draw needn't show every extreme that they name: Each row names two different experts. In each aligned block of 128 rows of routes[t, s] (the rows of one device), exactly 12 rows name expert s. An input is 256 consecutive token rows of a micro-batch; its first lengths tokens are live.
All inputs are finite; a program needn't handle non-finite values.
Results may differ from a plain program's by a relative error of at most 0.0045.
Values may be sent and summed in bfloat16 or wider, within the bound.
A program may use at most 64 MiB of HBM per device.

v0:
```python
import jax
import jax.numpy as jnp
from jax import lax
from jax.sharding import PartitionSpec as P

SEQ = 256


EPSILON = 1e-06


def shifted(x, axis, by):
    length = lax.axis_size(axis)
    return lax.ppermute(x, axis, [(i, (i + by) % length) for i in range(length)])


def normalize(hidden, gain_row):
    widened = hidden.astype(jnp.float32)
    mean_square = jnp.mean(widened * widened, axis=-1, keepdims=True)
    scaled = widened * lax.rsqrt(mean_square + EPSILON) * gain_row.astype(jnp.float32)[None, :]
    return (widened, scaled.astype(jnp.bfloat16))


def gate_pair(normed, router_matrix, chosen):
    logits = jnp.dot(normed, router_matrix, preferred_element_type=jnp.float32)
    expert_total = router_matrix.shape[1]
    picked = (
        chosen[:, :, None] == jnp.arange(expert_total, dtype=jnp.int32)[None, None, :]
    ).astype(jnp.float32)
    chosen_logits = jnp.sum(logits[:, None, :] * picked, axis=-1)
    first_gate = 1.0 / (1.0 + jnp.exp(chosen_logits[:, 1] - chosen_logits[:, 0]))
    second_gate = 1.0 / (1.0 + jnp.exp(chosen_logits[:, 0] - chosen_logits[:, 1]))
    return (first_gate, second_gate)


def device_layer(hidden, validity, chosen, weights, window, capacity):
    gain_row, router_matrix, up_local, down_local = weights
    widened, normed = normalize(hidden, gain_row)
    first_gate, second_gate = gate_pair(normed, router_matrix, chosen)
    first_hit = (chosen[:, 0] == window).astype(jnp.float32)
    second_hit = (chosen[:, 1] == window).astype(jnp.float32)
    weight_gate = first_gate * first_hit + second_gate * second_hit
    live_hit = (first_hit + second_hit) * validity
    slot_index = (jnp.cumsum(live_hit) - live_hit).astype(jnp.int32)
    target = jnp.where(live_hit > 0.5, slot_index, -1)
    slot_ids = jnp.arange(capacity, dtype=jnp.int32)[:, None]
    placing = (slot_ids == target[None, :]).astype(jnp.bfloat16)
    outgoing = jnp.dot(placing, normed, preferred_element_type=jnp.float32).astype(jnp.bfloat16)
    inner_sum = jnp.dot(
        lax.all_gather(outgoing, "expert", axis=0, tiled=True),
        up_local,
        preferred_element_type=jnp.float32,
    )
    activation = jax.nn.gelu(inner_sum).astype(jnp.bfloat16)
    terms = jnp.dot(activation, down_local, preferred_element_type=jnp.float32)
    summed = lax.psum_scatter(terms.astype(jnp.bfloat16), "expert", scatter_dimension=0, tiled=True)
    rows = lax.dot_general(
        placing, summed, (((0,), (0,)), ((), ())), preferred_element_type=jnp.float32
    )
    mixture = (weight_gate * live_hit)[:, None] * rows
    return (widened + mixture).astype(jnp.bfloat16)


def shards(stream, lengths, routes, norm_gains, router_weights, up_weights, down_weights):
    expert_rank = lax.axis_index("expert")
    section_rank = lax.axis_index("section")
    tok_rows = stream.shape[1]
    capacity = 3 * tok_rows // 32
    token_ids = expert_rank * tok_rows + jnp.arange(tok_rows, dtype=jnp.int32)
    owners = token_ids // SEQ
    offsets = token_ids % SEQ
    inputs_total = lengths.shape[1]
    matches = owners[:, None] == jnp.arange(inputs_total, dtype=jnp.int32)[None, :]
    own_length = jnp.sum(jnp.where(matches, lengths[0][None, :], 0), axis=1)
    validity = (offsets < own_length).astype(jnp.float32)
    weights = (norm_gains[0], router_weights[0], up_weights[0], down_weights[0])
    first_out = device_layer(stream[0], validity, routes[0, 0], weights, section_rank, capacity)
    moved, moved_valid = shifted((first_out, validity.astype(jnp.bfloat16)), "section", 1)
    keep_flag = (section_rank != 0).astype(jnp.float32)
    second_valid = moved_valid.astype(jnp.float32) * keep_flag
    second_out = device_layer(moved, second_valid, routes[1, 0], weights, section_rank, capacity)
    return second_out[None]


def solution(mesh):
    in_specs = (
        P("section", "expert", None),
        P("section", None),
        P(None, "section", "expert", None),
        P("section", None),
        P("section", None, None),
        P("section", None, "expert"),
        P("section", "expert", None),
    )
    out_specs = P("section", "expert", None)
    return jax.shard_map(shards, mesh=mesh, in_specs=in_specs, out_specs=out_specs, check_vma=False)
```

profile of v0, /device:TPU:102, one launch (start us, length us, event | category | flops | bytes accessed | tf_op | source)
XLA Modules:
  0.0 406.4 jit_solution(17327605617541800359)
XLA Ops:
  6.5 1.4 fusion.14
  8.0 0.7 select_reduce_fusion.2
  8.8 0.7 slice_bitcast_fusion
  9.5 0.7 convert_reduce_fusion
  10.2 1.6 fusion.25
  11.9 0.1 copy.26
  12.0 0.2 reduce-window.17
  12.1 0.1 reduce.1
  12.3 1.0 fusion.4
  13.3 0.0 all-gather.5.cloned.1.call-update
  13.3 0.0 all-gather.7.cloned.1.call-start
  13.3 74.7 %all-gather.5.cloned.1.call-done = bf16[32,12,2560]{2,1,0:T(8,128)(2,1)} async-done(((bf16[1,12,2560]{2,1,0:T(8,128)(2,1)}), bf16[32,12,2560]{2,1,0:T(8,128)(2,1)}) %all-gather.5.cloned.1.call-update) | async-done | bytes 1966096 | tf_op jit(solution)/shard_map/all_gather | solution.py:50
  88.1 4.0 reshape.225
  92.1 5.6 %convolution_convert_fusion.1 = bf16[384,2560]{1,0:T(8,128)(2,1)} fusion(bf16[1,320,2560]{2,1,0:T(8,128)(2,1)S(1)} %copy-done, bf16[384,2560]{1,0:T(8,128)(2,1)} %reshape.225, bf16[1,2560,320]{1,2,0:T(8,128)(2,1)} %param.12), kind=kOutput, calls=%fused_computation.1 | convolution fusion | flops 1260380160 | bytes 7208960 | tf_op jit(solution)/shard_map/dot_general | solution.py:55
  97.6 55.6 %fusion = bf16[16,2560]{1,0:T(8,128)(2,1)S(1)} fusion(bf16[384,2560]{1,0:T(8,128)(2,1)} %convolution_convert_fusion.1), kind=kCustom, calls=%all-reduce-scatter | all-reduce-scatter fusion | flops 1310721 | bytes 2050048
  153.2 4.2 %collective-permute-start.8 = (bf16[16,2560]{1,0:T(8,128)(2,1)S(1)}, bf16[16,2560]{1,0:T(8,128)(2,1)S(1)}, u32[]{:S(2)}, u32[]{:S(2)}) collective-permute-start(bf16[16,2560]{1,0:T(8,128)(2,1)S(1)} %fusion), channel_id=1, source_target_pairs={{0,7},{1,8},{2,9},{3,10},{4,11},{5,12},{6,13},{7,14},{8,15},{9,16}... | collective-permute-start | bytes 245768
  157.4 3.8 collective-permute-start.7
  161.3 4.4 %collective-permute-start.9 = (bf16[12,2560]{1,0:T(8,128)(2,1)S(1)}, bf16[12,2560]{1,0:T(8,128)(2,1)S(1)}, u32[]{:S(2)}, u32[]{:S(2)}) collective-permute-start(bf16[12,2560]{1,0:T(8,128)(2,1)S(1)} %slice.44), channel_id=1, source_target_pairs={{0,8},{1,9},{2,10},{3,11},{4,12},{5,13},{6,14},{7,15},{8,16},{9,17... | collective-permute-start | bytes 184328
  165.7 6.7 %collective-permute-start.6 = (bf16[16,2560]{1,0:T(8,128)(2,1)S(1)}, bf16[16,2560]{1,0:T(8,128)(2,1)S(1)}, u32[]{:S(2)}, u32[]{:S(2)}) collective-permute-start(bf16[16,2560]{1,0:T(8,128)(2,1)S(1)} %fusion), channel_id=1, source_target_pairs={{0,5},{1,6},{2,7},{3,8},{4,9},{5,10},{6,11},{7,12},{8,13},{9,14},{... | collective-permute-start | bytes 245768
  172.4 2.5 collective-permute-start.5
  174.8 2.3 collective-permute-done.9
  177.2 1.9 collective-permute-start.4
  179.1 0.0 collective-permute-done.8
  179.1 6.6 %collective-permute-start.3 = (bf16[16,2560]{1,0:T(8,128)(2,1)S(1)}, bf16[16,2560]{1,0:T(8,128)(2,1)S(1)}, u32[]{:S(2)}, u32[]{:S(2)}) collective-permute-start(bf16[16,2560]{1,0:T(8,128)(2,1)S(1)} %fusion), channel_id=1, source_target_pairs={{0,2},{1,3},{2,4},{3,5},{4,6},{5,7},{6,8},{7,9},{8,10},{9,11},{10,... | collective-permute-start | bytes 245768
  185.7 0.0 collective-permute-done.7
  185.7 2.8 collective-permute-start.2
  188.5 1.3 dynamic-slice.6
  190.4 0.0 copy-start.2
  190.4 0.6 copy-done.2
  191.1 0.6 copy-done.3
  191.7 0.3 collective-permute-done.2
  192.0 4.1 %concatenate = bf16[140,2560]{1,0:T(8,128)(2,1)S(1)} concatenate(bf16[12,2560]{1,0:T(8,128)(2,1)S(1)} %collective-permute-done.9, bf16[16,2560]{1,0:T(8,128)(2,1)S(1)} %collective-permute-done.8, bf16[16,2560]{1,0:T(8,128)(2,1)S(1)} %collective-permute-done.7, bf16[16,2560]{1,0:T(8,128)(2,1)S(1)} %collective-permute-done.6, bf16[16,2560]{1,0:T(8,128)(2,1)S(1)} %collective-permute-done.5, ...), dimensions={0} | concatenate | bytes 1433600
  196.1 0.0 copy-start.6
  196.1 1.2 fusion.3
  197.4 3.4 collective-permute-start
  200.8 3.4 collective-permute-start.1
  204.2 14.3 %collective-permute-done = bf16[128,2560]{1,0:T(8,128)(2,1)S(1)} collective-permute-done((bf16[128,2560]{1,0:T(8,128)(2,1)}, bf16[128,2560]{1,0:T(8,128)(2,1)S(1)}, u32[]{:S(2)}, u32[]{:S(2)}) %collective-permute-start) | collective-permute-done | bytes 655392 | tf_op jit(solution)/shard_map/ppermute | solution.py:14
  218.5 0.2 fusion.19
  218.7 0.4 fusion.60
  219.2 0.1 copy.27
  219.3 0.2 reduce-window.18
  219.4 0.1 reduce.2
  219.6 1.0 fusion.5
  220.5 0.0 all-gather.7.cloned.1.call-update
  220.6 69.7 %all-gather.7.cloned.1.call-done = bf16[32,12,2560]{2,1,0:T(8,128)(2,1)} async-done(((bf16[1,12,2560]{2,1,0:T(8,128)(2,1)}), bf16[32,12,2560]{2,1,0:T(8,128)(2,1)}) %all-gather.7.cloned.1.call-update) | async-done | bytes 1966096 | tf_op jit(solution)/shard_map/all_gather | solution.py:50
  290.2 4.0 reshape.227
  294.2 5.6 %convolution_convert_fusion = bf16[384,2560]{1,0:T(8,128)(2,1)} fusion(bf16[1,320,2560]{2,1,0:T(8,128)(2,1)S(1)} %copy-done, bf16[384,2560]{1,0:T(8,128)(2,1)} %reshape.227, bf16[1,2560,320]{1,2,0:T(8,128)(2,1)} %param.12), kind=kOutput, calls=%fused_computation | convolution fusion | flops 1260380160 | bytes 7208960 | tf_op jit(solution)/shard_map/dot_general | solution.py:55
  299.8 55.6 %fusion.1 = bf16[16,2560]{1,0:T(8,128)(2,1)S(1)} fusion(bf16[384,2560]{1,0:T(8,128)(2,1)} %convolution_convert_fusion), kind=kCustom, calls=%all-reduce-scatter.1 | all-reduce-scatter fusion | flops 1310721 | bytes 2050048
  355.4 4.2 %collective-permute-start.16 = (bf16[16,2560]{1,0:T(8,128)(2,1)S(1)}, bf16[16,2560]{1,0:T(8,128)(2,1)S(1)}, u32[]{:S(2)}, u32[]{:S(2)}) collective-permute-start(bf16[16,2560]{1,0:T(8,128)(2,1)S(1)} %fusion.1), channel_id=1, source_target_pairs={{0,7},{1,8},{2,9},{3,10},{4,11},{5,12},{6,13},{7,14},{8,15},{9,16}... | collective-permute-start | bytes 245768
  359.6 3.8 collective-permute-start.15
  363.4 4.4 %collective-permute-start.17 = (bf16[12,2560]{1,0:T(8,128)(2,1)S(1)}, bf16[12,2560]{1,0:T(8,128)(2,1)S(1)}, u32[]{:S(2)}, u32[]{:S(2)}) collective-permute-start(bf16[12,2560]{1,0:T(8,128)(2,1)S(1)} %slice.45), channel_id=1, source_target_pairs={{0,8},{1,9},{2,10},{3,11},{4,12},{5,13},{6,14},{7,15},{8,16},{9,17... | collective-permute-start | bytes 184328
  367.8 6.7 %collective-permute-start.14 = (bf16[16,2560]{1,0:T(8,128)(2,1)S(1)}, bf16[16,2560]{1,0:T(8,128)(2,1)S(1)}, u32[]{:S(2)}, u32[]{:S(2)}) collective-permute-start(bf16[16,2560]{1,0:T(8,128)(2,1)S(1)} %fusion.1), channel_id=1, source_target_pairs={{0,5},{1,6},{2,7},{3,8},{4,9},{5,10},{6,11},{7,12},{8,13},{9,14},{... | collective-permute-start | bytes 245768
  374.5 2.5 collective-permute-start.13
  377.0 2.3 collective-permute-done.17
  379.4 1.9 collective-permute-start.12
  381.3 6.6 %collective-permute-start.11 = (bf16[16,2560]{1,0:T(8,128)(2,1)S(1)}, bf16[16,2560]{1,0:T(8,128)(2,1)S(1)}, u32[]{:S(2)}, u32[]{:S(2)}) collective-permute-start(bf16[16,2560]{1,0:T(8,128)(2,1)S(1)} %fusion.1), channel_id=1, source_target_pairs={{0,2},{1,3},{2,4},{3,5},{4,6},{5,7},{6,8},{7,9},{8,10},{9,11},{10,... | collective-permute-start | bytes 245768
  387.9 2.8 collective-permute-start.10
  390.7 0.0 copy-start.4
  390.7 0.5 collective-permute-done.11
  391.2 0.1 copy-done.4
  391.3 0.6 copy-done.5
  391.9 2.3 collective-permute-done.10
  394.2 4.1 %concatenate.1 = bf16[140,2560]{1,0:T(8,128)(2,1)S(1)} concatenate(bf16[12,2560]{1,0:T(8,128)(2,1)S(1)} %collective-permute-done.17, bf16[16,2560]{1,0:T(8,128)(2,1)S(1)} %collective-permute-done.16, bf16[16,2560]{1,0:T(8,128)(2,1)S(1)} %collective-permute-done.15, bf16[16,2560]{1,0:T(8,128)(2,1)S(1)} %collective-permute-done.14, bf16[16,2560]{1,0:T(8,128)(2,1)S(1)} %collective-permute-done.13, ...), dimensions={0} | concatenate | bytes 1433600
  398.3 1.2 fusion.23
  (30 shorter events, 0.2 us)
Async XLA Ops:
  6.5 85.5 %copy-start = (bf16[1,320,2560]{2,1,0:T(8,128)(2,1)S(1)}, bf16[1,320,2560]{2,1,0:T(8,128)(2,1)}, u32[]{:S(2)}) copy-start(bf16[1,320,2560]{2,1,0:T(8,128)(2,1)} %param.13) | copy-start | bytes 4915204
  6.5 5.7 %copy-start.1 = (bf16[1,128,2560]{2,1,0:T(8,128)(2,1)S(1)}, bf16[1,128,2560]{2,1,0:T(8,128)(2,1)}, u32[]{:S(2)}) copy-start(bf16[1,128,2560]{2,1,0:T(8,128)(2,1)} %param.7) | copy-start | bytes 1966084
  6.5 81.5 %all-gather.5.cloned.1.call-start = ((), (), s32[]{:S(2)}) async-start(), calls=%async_computation | async-start | bytes 2703360 | tf_op jit(solution)/shard_map/all_gather | solution.py:50
  13.3 276.9 %all-gather.7.cloned.1.call-start = ((), (), s32[]{:S(2)}) async-start(), calls=%async_computation.1 | async-start | bytes 2703360 | tf_op jit(solution)/shard_map/all_gather | solution.py:50
  153.2 25.9 %collective-permute-start.8 = (bf16[16,2560]{1,0:T(8,128)(2,1)S(1)}, bf16[16,2560]{1,0:T(8,128)(2,1)S(1)}, u32[]{:S(2)}, u32[]{:S(2)}) collective-permute-start(bf16[16,2560]{1,0:T(8,128)(2,1)S(1)} %fusion), channel_id=1, source_target_pairs={{0,7},{1,8},{2,9},{3,10},{4,11},{5,12},{6,13},{7,14},{8,15},{9,16}... | collective-permute-start | bytes 245768
  157.4 28.3 %collective-permute-start.7 = (bf16[16,2560]{1,0:T(8,128)(2,1)S(1)}, bf16[16,2560]{1,0:T(8,128)(2,1)S(1)}, u32[]{:S(2)}, u32[]{:S(2)}) collective-permute-start(bf16[16,2560]{1,0:T(8,128)(2,1)S(1)} %fusion), channel_id=1, source_target_pairs={{0,6},{1,7},{2,8},{3,9},{4,10},{5,11},{6,12},{7,13},{8,14},{9,15},... | collective-permute-start | bytes 245768
  161.3 15.9 %collective-permute-start.9 = (bf16[12,2560]{1,0:T(8,128)(2,1)S(1)}, bf16[12,2560]{1,0:T(8,128)(2,1)S(1)}, u32[]{:S(2)}, u32[]{:S(2)}) collective-permute-start(bf16[12,2560]{1,0:T(8,128)(2,1)S(1)} %slice.44), channel_id=1, source_target_pairs={{0,8},{1,9},{2,10},{3,11},{4,12},{5,13},{6,14},{7,15},{8,16},{9,17... | collective-permute-start | bytes 184328
  165.7 24.7 %collective-permute-start.6 = (bf16[16,2560]{1,0:T(8,128)(2,1)S(1)}, bf16[16,2560]{1,0:T(8,128)(2,1)S(1)}, u32[]{:S(2)}, u32[]{:S(2)}) collective-permute-start(bf16[16,2560]{1,0:T(8,128)(2,1)S(1)} %fusion), channel_id=1, source_target_pairs={{0,5},{1,6},{2,7},{3,8},{4,9},{5,10},{6,11},{7,12},{8,13},{9,14},{... | collective-permute-start | bytes 245768
  172.4 18.0 %collective-permute-start.5 = (bf16[16,2560]{1,0:T(8,128)(2,1)S(1)}, bf16[16,2560]{1,0:T(8,128)(2,1)S(1)}, u32[]{:S(2)}, u32[]{:S(2)}) collective-permute-start(bf16[16,2560]{1,0:T(8,128)(2,1)S(1)} %fusion), channel_id=1, source_target_pairs={{0,4},{1,5},{2,6},{3,7},{4,8},{5,9},{6,10},{7,11},{8,12},{9,13},{1... | collective-permute-start | bytes 245768
  177.2 13.2 %collective-permute-start.4 = (bf16[16,2560]{1,0:T(8,128)(2,1)S(1)}, bf16[16,2560]{1,0:T(8,128)(2,1)S(1)}, u32[]{:S(2)}, u32[]{:S(2)}) collective-permute-start(bf16[16,2560]{1,0:T(8,128)(2,1)S(1)} %fusion), channel_id=1, source_target_pairs={{0,3},{1,4},{2,5},{3,6},{4,7},{5,8},{6,9},{7,10},{8,11},{9,12},{10... | collective-permute-start | bytes 245768
  179.1 11.3 %collective-permute-start.3 = (bf16[16,2560]{1,0:T(8,128)(2,1)S(1)}, bf16[16,2560]{1,0:T(8,128)(2,1)S(1)}, u32[]{:S(2)}, u32[]{:S(2)}) collective-permute-start(bf16[16,2560]{1,0:T(8,128)(2,1)S(1)} %fusion), channel_id=1, source_target_pairs={{0,2},{1,3},{2,4},{3,5},{4,6},{5,7},{6,8},{7,9},{8,10},{9,11},{10,... | collective-permute-start | bytes 245768
  185.7 6.3 %collective-permute-start.2 = (bf16[16,2560]{1,0:T(8,128)(2,1)S(1)}, bf16[16,2560]{1,0:T(8,128)(2,1)}, u32[]{:S(2)}, u32[]{:S(2)}) collective-permute-start(bf16[16,2560]{1,0:T(8,128)(2,1)S(1)} %fusion), channel_id=1, source_target_pairs={{0,1},{1,2},{2,3},{3,4},{4,5},{5,6},{6,7},{7,8},{8,9},{9,10},{10,1... | collective-permute-start | bytes 245768
  190.4 0.6 copy-start.2
  191.1 0.6 copy-start.3
  196.1 22.5 %copy-start.6 = (bf16[1,2560,64]{1,2,0:T(8,128)(2,1)S(1)}, bf16[1,2560,64]{1,2,0:T(8,128)(2,1)}, u32[]{:S(2)}) copy-start(bf16[1,2560,64]{1,2,0:T(8,128)(2,1)} %param.11) | copy-start | bytes 983044
  197.4 21.1 %collective-permute-start = (bf16[128,2560]{1,0:T(8,128)(2,1)}, bf16[128,2560]{1,0:T(8,128)(2,1)S(1)}, u32[]{:S(2)}, u32[]{:S(2)}) collective-permute-start(bf16[128,2560]{1,0:T(8,128)(2,1)} %fusion.3), channel_id=1, source_target_pairs={{0,32},{32,64},{64,96},{96,128},{128,160},{160,192},{192,224},{224... | collective-permute-start | bytes 1966088 | tf_op jit(solution)/shard_map/ppermute | solution.py:14
  200.8 18.4 %collective-permute-start.1 = (bf16[128]{0:T(256)(128)(2,1)S(1)}, bf16[128]{0:T(256)(128)(2,1)S(1)}, u32[]{:S(2)}, u32[]{:S(2)}) collective-permute-start(bf16[128]{0:T(256)(128)(2,1)S(1)} %get-tuple-element.7), channel_id=1, source_target_pairs={{0,32},{32,64},{64,96},{96,128},{128,160},{160,192},{192,224},{224... | collective-permute-start | bytes 776 | tf_op jit(solution)/shard_map/ppermute | solution.py:14
  355.4 25.9 %collective-permute-start.16 = (bf16[16,2560]{1,0:T(8,128)(2,1)S(1)}, bf16[16,2560]{1,0:T(8,128)(2,1)S(1)}, u32[]{:S(2)}, u32[]{:S(2)}) collective-permute-start(bf16[16,2560]{1,0:T(8,128)(2,1)S(1)} %fusion.1), channel_id=1, source_target_pairs={{0,7},{1,8},{2,9},{3,10},{4,11},{5,12},{6,13},{7,14},{8,15},{9,16}... | collective-permute-start | bytes 245768
  359.6 28.3 %collective-permute-start.15 = (bf16[16,2560]{1,0:T(8,128)(2,1)S(1)}, bf16[16,2560]{1,0:T(8,128)(2,1)S(1)}, u32[]{:S(2)}, u32[]{:S(2)}) collective-permute-start(bf16[16,2560]{1,0:T(8,128)(2,1)S(1)} %fusion.1), channel_id=1, source_target_pairs={{0,6},{1,7},{2,8},{3,9},{4,10},{5,11},{6,12},{7,13},{8,14},{9,15},... | collective-permute-start | bytes 245768
  363.4 15.9 %collective-permute-start.17 = (bf16[12,2560]{1,0:T(8,128)(2,1)S(1)}, bf16[12,2560]{1,0:T(8,128)(2,1)S(1)}, u32[]{:S(2)}, u32[]{:S(2)}) collective-permute-start(bf16[12,2560]{1,0:T(8,128)(2,1)S(1)} %slice.45), channel_id=1, source_target_pairs={{0,8},{1,9},{2,10},{3,11},{4,12},{5,13},{6,14},{7,15},{8,16},{9,17... | collective-permute-start | bytes 184328
  367.8 22.8 %collective-permute-start.14 = (bf16[16,2560]{1,0:T(8,128)(2,1)S(1)}, bf16[16,2560]{1,0:T(8,128)(2,1)S(1)}, u32[]{:S(2)}, u32[]{:S(2)}) collective-permute-start(bf16[16,2560]{1,0:T(8,128)(2,1)S(1)} %fusion.1), channel_id=1, source_target_pairs={{0,5},{1,6},{2,7},{3,8},{4,9},{5,10},{6,11},{7,12},{8,13},{9,14},{... | collective-permute-start | bytes 245768
  374.5 16.1 %collective-permute-start.13 = (bf16[16,2560]{1,0:T(8,128)(2,1)S(1)}, bf16[16,2560]{1,0:T(8,128)(2,1)S(1)}, u32[]{:S(2)}, u32[]{:S(2)}) collective-permute-start(bf16[16,2560]{1,0:T(8,128)(2,1)S(1)} %fusion.1), channel_id=1, source_target_pairs={{0,4},{1,5},{2,6},{3,7},{4,8},{5,9},{6,10},{7,11},{8,12},{9,13},{1... | collective-permute-start | bytes 245768
  379.4 11.3 %collective-permute-start.12 = (bf16[16,2560]{1,0:T(8,128)(2,1)S(1)}, bf16[16,2560]{1,0:T(8,128)(2,1)S(1)}, u32[]{:S(2)}, u32[]{:S(2)}) collective-permute-start(bf16[16,2560]{1,0:T(8,128)(2,1)S(1)} %fusion.1), channel_id=1, source_target_pairs={{0,3},{1,4},{2,5},{3,6},{4,7},{5,8},{6,9},{7,10},{8,11},{9,12},{10... | collective-permute-start | bytes 245768
  381.3 9.9 %collective-permute-start.11 = (bf16[16,2560]{1,0:T(8,128)(2,1)S(1)}, bf16[16,2560]{1,0:T(8,128)(2,1)S(1)}, u32[]{:S(2)}, u32[]{:S(2)}) collective-permute-start(bf16[16,2560]{1,0:T(8,128)(2,1)S(1)} %fusion.1), channel_id=1, source_target_pairs={{0,2},{1,3},{2,4},{3,5},{4,6},{5,7},{6,8},{7,9},{8,10},{9,11},{10,... | collective-permute-start | bytes 245768
  387.9 6.3 %collective-permute-start.10 = (bf16[16,2560]{1,0:T(8,128)(2,1)S(1)}, bf16[16,2560]{1,0:T(8,128)(2,1)}, u32[]{:S(2)}, u32[]{:S(2)}) collective-permute-start(bf16[16,2560]{1,0:T(8,128)(2,1)S(1)} %fusion.1), channel_id=1, source_target_pairs={{0,1},{1,2},{2,3},{3,4},{4,5},{5,6},{6,7},{7,8},{8,9},{9,10},{10,1... | collective-permute-start | bytes 245768
  390.7 0.6 copy-start.4
  391.3 0.6 copy-start.5
Sparse Core Ops, SparseCore 0:
  13.4 74.6 all-gather.4
  220.7 69.4 all-gather.6
where the time goes:
time: 408 us; the launch traced here: 406 us
  waiting for transfers between devices  167 us (41%)
  blocking collectives  111 us (27%)
  starting transfers between devices  72.3 us (18%)
  local copies, waits for them, and re-layouts  20.5 us (5%)
  matrix products  17.5 us (4%)
  between operations  14.5 us (4%)
    all_gather x2, waiting for transfers between devices, device_layer(): lax.all_gather(outgoing, 'expert', axis=0, tiled=True)  144 us
    unnamed x2, blocking collectives  111 us
    unnamed x16, starting transfers between devices  65.5 us
    unnamed x21, local copies, waits for them, and re-layouts  19.6 us
    ppermute x2, waiting for transfers between devices, shifted(): lax.ppermute(x, axis, [(i, (i + by) % length) for i in range(length)])  14.3 us
    dot_general x2, matrix products, device_layer(): terms = jnp.dot(activation, down_local, preferred_element_type=jnp.float32)  11.1 us
  transfers between devices with their start and end apart: 20, of which 8 were waited for; matrix products, arithmetic and copies ran while one was open for 0% of the time, Pallas kernels for 0%

commit v1 on v0

v1 whole, which is shorter than its diff:
```python
import functools

import jax
import jax.numpy as jnp
from jax import lax
from jax.experimental import pallas as pl
from jax.experimental.pallas import tpu as pltpu
from jax.sharding import PartitionSpec as P

MESH = pl.DeviceIdType.MESH
EPSILON = 1e-06
CAPACITY = 12

CHILDREN = {0: (2, 1), 2: (4, 3), 4: (6, 5), 6: (8, 7)}
STAGES = (((2,), (1,)), ((4,), (3,)), ((6,), (5,)), ((), (7, 8)))
PARENT = {child: node for node, kids in CHILDREN.items() for child in kids}
FAR = 8


def slot_order():
    order, groups = [(0, 1)], []
    for inner, leaves in STAGES:
        first = len(order) if groups else 0
        for node in inner + leaves:
            order += [(node, 1)] if node == FAR else [(node, 1), (node, -1)]
        groups.append((first, len(order)))
    places = {pair: place for place, pair in enumerate(order)}
    places[(FAR, -1)] = places[(FAR, 1)]
    places[(0, -1)] = 0
    return places, groups


PLACE, GROUPS = slot_order()
OFFSETS = sorted({sign * (child - node) for child, node in PARENT.items() for sign in (1, -1)})


def body(
    sizes,
    stream_ref, lengths_ref, routes_ref, gains_ref, router_ref, up_ref, down_ref,
    out_ref,
    held, held_prev, merged, info, info_prev, up_own, up_other, up_joint, down_all, router_all,
    gathered, unpacked, hidden, raw, packed_sums, outgoing, incoming, finished, finished_prev, staged,
    local_sem, swap_send, swap_recv, shift_send, shift_recv,
    gather_send, gather_recv, reduce_send, reduce_recv, out_sem,
):
    sections, ranks, rows, width, own_hidden = sizes
    main = width // 4 * 3
    part = main // 3
    half = 8 * 128
    wide = own_hidden // 256 * 256
    rest = own_hidden - wide
    section = lax.axis_index("section")
    rank = lax.axis_index("expert")
    chip, core = rank // 2, lax.rem(rank, 2)
    sibling = (section, rank + 1 - 2 * core)
    following = (lax.rem(section + 1, sections), rank)
    previous = (lax.rem(section + sections - 1, sections), rank)

    def along(steps):
        return (section, lax.rem(rank + 2 * steps + ranks, ranks))

    def columns(node, sign):
        if node != FAR:
            return pl.ds(0, main)
        return pl.ds(0, half) if sign > 0 else pl.ds(half, main - half)

    def remote(src, dst, send, recv, device):
        return pltpu.make_async_remote_copy(
            src_ref=src, dst_ref=dst, send_sem=send, recv_sem=recv, device_id=device, device_id_type=MESH
        )

    loads = [
        pltpu.make_async_copy(stream_ref.at[0], held, local_sem.at[0]),
        pltpu.make_async_copy(router_ref.at[0], router_all, local_sem.at[1]),
        pltpu.make_async_copy(up_ref.at[0], up_own, local_sem.at[2]),
        pltpu.make_async_copy(down_ref.at[0, pl.ds(0, wide)], down_all.at[pl.ds(0, wide)], local_sem.at[3]),
        pltpu.make_async_copy(
            down_ref.at[0, pl.ds(wide, rest)], down_all.at[pl.ds(2 * wide, rest)], local_sem.at[4]
        ),
    ]
    for load in loads:
        load.start()

    barrier = pltpu.get_barrier_semaphore()
    peers = [along(offset) for offset in OFFSETS] + [sibling, following, previous]
    for peer in peers:
        pl.semaphore_signal(barrier, inc=1, device_id=peer, device_id_type=MESH)

    lane = lax.broadcasted_iota(jnp.int32, (rows, rows), 1)
    row = lax.broadcasted_iota(jnp.int32, (rows, rows), 0)
    before = (row > lane).astype(jnp.bfloat16)
    slot_row = lax.broadcasted_iota(jnp.int32, (16, part), 0)
    gain = gains_ref[...].astype(jnp.float32)

    def pack(value):
        tail = value[:, main:]
        pieces = []
        for i in range(3):
            moved = pltpu.roll(tail, 12 - 4 * i, 0)
            pieces.append(jnp.where(slot_row < CAPACITY, value[:, i * part : (i + 1) * part], moved))
        return pieces

    def tail_of(pieces):
        result = pltpu.roll(pieces[0], 4, 0)
        result = jnp.where(slot_row < 4, result, pltpu.roll(pieces[1], 8, 0))
        result = jnp.where(slot_row < 8, result, pltpu.roll(pieces[2], 12, 0))
        return result

    def placing(chosen, validity):
        first = jnp.broadcast_to(chosen[:, 0:1], (rows, rows))
        second = jnp.broadcast_to(chosen[:, 1:2], (rows, rows))
        hit = ((first == section) | (second == section)).astype(jnp.float32) * validity
        slot = jnp.dot(before, hit.astype(jnp.bfloat16), preferred_element_type=jnp.float32)
        spread = jnp.where((slot == lane.astype(jnp.float32)) & (hit > 0.5), 1.0, 0.0)
        return first, second, hit, spread, jnp.transpose(spread)

    def normalize(x):
        mean_square = jnp.sum(x * x, axis=-1, keepdims=True) * (1.0 / width)
        return x * lax.rsqrt(mean_square + EPSILON) * gain

    def gates(normed, picking, first, second):
        logits = jnp.dot(normed, router_all[...], preferred_element_type=jnp.float32)
        experts = logits.shape[1]
        ids = lax.broadcasted_iota(jnp.int32, logits.shape, 1).astype(jnp.float32)
        chosen = [
            jnp.dot(picking, q.astype(jnp.float32).astype(jnp.bfloat16), preferred_element_type=jnp.float32)[:, :experts]
            for q in (first, second)
        ]
        a, b = (jnp.sum(jnp.where(ids == q, logits, 0.0), axis=-1, keepdims=True) for q in chosen)
        first_gate = 1.0 / (1.0 + jnp.exp(b - a))
        second_gate = 1.0 / (1.0 + jnp.exp(a - b))
        mine = section.astype(jnp.float32)
        return jnp.where(
            chosen[0][:, 0:1] == mine, first_gate, jnp.where(chosen[1][:, 0:1] == mine, second_gate, 0.0)
        )

    def gather_copy(tick, node, child, sign):
        cols = columns(child, sign)
        way = 0 if sign > 0 else 1
        return remote(
            gathered.at[tick, PLACE[(node, sign)], :, cols],
            gathered.at[tick, PLACE[(child, sign)], :, cols],
            gather_send.at[tick, way, child],
            gather_recv.at[tick, way, child],
            along(sign * (child - node)),
        )

    def reduce_copy(tick, child, sign):
        cols = columns(child, sign)
        way = 0 if sign > 0 else 1
        return remote(
            outgoing.at[tick, way, child, :, cols],
            incoming.at[tick, way, child, :, cols],
            reduce_send.at[tick, way, child],
            reduce_recv.at[tick, way, child],
            along(sign * (child - PARENT[child])),
        )

    def forward(tick, node):
        for child in CHILDREN.get(node, ()):
            for sign in (1, -1):
                gather_copy(tick, node, child, sign).start()

    def expert(tick, first, last):
        low, count = 16 * first, 16 * (last - first)
        for place in range(first, last):
            at = pl.ds(16 * place, 16)
            block = gathered[tick, place]
            unpacked[at, 0:main] = block
            wider = block.astype(jnp.float32)
            tail = tail_of([wider[:, i * part : (i + 1) * part] for i in range(3)])
            unpacked[at, main:width] = tail.astype(jnp.bfloat16)
        at = pl.ds(low, count)
        tokens = unpacked[at, :]
        for begin, matrix in ((0, up_own[:, 0:wide]), (wide, up_other[:, 0:wide]), (2 * wide, up_joint[...])):
            inner = jnp.dot(tokens, matrix, preferred_element_type=jnp.float32)
            hidden[at, begin : begin + inner.shape[1]] = jax.nn.gelu(inner).astype(jnp.bfloat16)
        active = hidden[at, :]
        for begin in range(0, width, 512):
            raw[at, begin : begin + 512] = jnp.dot(
                active, down_all[:, begin : begin + 512], preferred_element_type=jnp.float32
            )
        for place in range(first, last):
            for i, piece in enumerate(pack(raw[pl.ds(16 * place, 16), :])):
                packed_sums[place, :, i * part : (i + 1) * part] = piece

    def send_sum(tick, node, sign):
        way = 0 if sign > 0 else 1
        cols = columns(node, sign)
        for child in CHILDREN.get(node, ()):
            reduce_copy(tick, child, sign).wait_recv()
        if FAR in CHILDREN.get(node, ()):
            other = [child for child in CHILDREN[node] if child != FAR]
            for near, far_cols in ((True, columns(FAR, sign)), (False, columns(FAR, -sign))):
                value = packed_sums[PLACE[(node, -sign)], :, far_cols]
                for child in other + ([FAR] if near else []):
                    value = value + incoming[tick, way, child, :, far_cols].astype(jnp.float32)
                outgoing[tick, way, node, :, far_cols] = value.astype(jnp.bfloat16)
        else:
            total = packed_sums[PLACE[(node, -sign)], :, cols]
            for child in CHILDREN.get(node, ()):
                total = total + incoming[tick, way, child, :, cols].astype(jnp.float32)
            outgoing[tick, way, node, :, cols] = total.astype(jnp.bfloat16)
        reduce_copy(tick, node, sign).start()

    def mixture(tick, normed, meanwhile, weights_ready=None):
        for i, piece in enumerate(pack(normed)):
            gathered[tick, 0, :, i * part : (i + 1) * part] = piece.astype(jnp.bfloat16)
        forward(tick, 0)
        meanwhile()
        for (inner, leaves), (first, last) in zip(STAGES, GROUPS):
            for node in inner:
                for sign in (1, -1):
                    gather_copy(tick, PARENT[node], node, sign).wait_recv()
                forward(tick, node)
            for node in leaves:
                for sign in (1, -1):
                    gather_copy(tick, PARENT[node], node, sign).wait_recv()
            if first == 0 and weights_ready:
                weights_ready()
            expert(tick, first, last)
            for node in leaves:
                for sign in (1, -1):
                    send_sum(tick, node, sign)
        for inner, _ in reversed(STAGES):
            for node in inner:
                for sign in (1, -1):
                    send_sum(tick, node, sign)
        total = packed_sums[0]
        for child in CHILDREN[0]:
            for sign in (1, -1):
                reduce_copy(tick, child, sign).wait_recv()
        for child in CHILDREN[0]:
            for way in (0, 1):
                total = total + incoming[tick, way, child].astype(jnp.float32)
        pieces = [total[:, i * part : (i + 1) * part] for i in range(3)]
        keep = slot_row < CAPACITY
        summed = jnp.concatenate([jnp.where(keep, p, 0.0) for p in pieces] + [jnp.where(keep, tail_of(pieces), 0.0)], axis=1)
        return summed.astype(jnp.bfloat16).astype(jnp.float32)

    own_length = lengths_ref[0, chip]
    validity = ((core * rows + row) < own_length).astype(jnp.float32)
    first, second, _, spread, picked = placing(routes_ref[0, 0], validity)
    info[...] = jnp.where(lane < 16, spread, validity).astype(jnp.bfloat16)
    picking = picked[0:16].astype(jnp.bfloat16)
    loads[0].wait()
    x = jnp.dot(picking, held[...], preferred_element_type=jnp.float32)
    normed = normalize(x).astype(jnp.bfloat16)
    pl.semaphore_wait(barrier, len(peers))

    swaps = [
        remote(up_ref.at[0], up_other, swap_send.at[0], swap_recv.at[0], sibling),
        remote(
            down_ref.at[0, pl.ds(0, wide)], down_all.at[pl.ds(wide, wide)], swap_send.at[1], swap_recv.at[1], sibling
        ),
        remote(
            down_ref.at[0, pl.ds(wide, rest)],
            down_all.at[pl.ds(2 * wide + rest, rest)],
            swap_send.at[2],
            swap_recv.at[2],
            sibling,
        ),
    ]
    shifts = [
        remote(info, info_prev, shift_send.at[0], shift_recv.at[0], following),
        remote(stream_ref.at[0], held_prev, shift_send.at[1], shift_recv.at[1], following),
        remote(finished, finished_prev, shift_send.at[2], shift_recv.at[2], following),
    ]
    gate = [None, None]

    def first_meanwhile():
        for copy in swaps + shifts[:2]:
            copy.start()
        loads[1].wait()
        gate[0] = gates(normed, picking, first, second)

    def weights_ready():
        for load in loads[2:]:
            load.wait()
        for copy in swaps:
            copy.wait_recv()
        up_joint[...] = jnp.concatenate([up_own[:, wide:], up_other[:, wide:]], axis=1)

    summed = mixture(0, normed.astype(jnp.float32), first_meanwhile, weights_ready)
    for i, piece in enumerate(pack(x + gate[0] * summed)):
        finished[:, i * part : (i + 1) * part] = piece.astype(jnp.bfloat16)
    shifts[2].start()

    shifts[0].wait_recv()
    prior = info_prev[...].astype(jnp.float32)
    live = jnp.broadcast_to(prior[:, 64:65], (rows, rows)) * (section != 0).astype(jnp.float32)
    prior_spread = jnp.where(lane < 16, prior, 0.0)
    prior_picked = jnp.transpose(prior_spread)
    renewed_row = jnp.sum(prior_picked, axis=0, keepdims=True)
    renewed = jnp.sum(prior_spread, axis=1, keepdims=True)
    first2, second2, hit2, spread2, picked2 = placing(routes_ref[1, 0], live)
    picking2 = picked2[0:16].astype(jnp.bfloat16)
    old_rows = (picked2[0:16] * (1.0 - renewed_row)).astype(jnp.bfloat16)
    new_rows = jnp.dot(picking2, prior_spread.astype(jnp.bfloat16), preferred_element_type=jnp.float32)
    new_rows = new_rows[:, 0:16].astype(jnp.bfloat16)
    shifts[1].wait_recv()
    kept = jnp.dot(old_rows, held_prev[...], preferred_element_type=jnp.float32)

    shifts[2].wait_recv()
    block = finished_prev[...].astype(jnp.float32)
    pieces = [block[:, i * part : (i + 1) * part] for i in range(3)]
    keep = slot_row < CAPACITY
    update = jnp.concatenate(
        [jnp.where(keep, p, 0.0) for p in pieces] + [jnp.where(keep, tail_of(pieces), 0.0)], axis=1
    ).astype(jnp.bfloat16)
    x2 = kept + jnp.dot(new_rows, update, preferred_element_type=jnp.float32)
    normed2 = normalize(x2).astype(jnp.bfloat16)

    def second_meanwhile():
        gate[1] = gates(normed2, picking2, first2, second2)
        placed = jnp.dot(
            prior_spread[:, 0:16].astype(jnp.bfloat16), update, preferred_element_type=jnp.float32
        ).astype(jnp.bfloat16)
        merged[...] = jnp.where(renewed > 0.5, placed, held_prev[...])

    summed2 = mixture(1, normed2.astype(jnp.float32), second_meanwhile)
    final = (x2 + gate[1] * summed2).astype(jnp.bfloat16)
    spread_final = spread2[:, 0:16].astype(jnp.bfloat16)
    struck = hit2[:, 0:1] > 0.5
    stores = []
    for i in range(4):
        cols = pl.ds(i * part, part)
        placed = jnp.dot(spread_final, final[:, i * part : (i + 1) * part], preferred_element_type=jnp.float32)
        staged[:, cols] = jnp.where(struck, placed.astype(jnp.bfloat16), merged[:, cols])
        store = pltpu.make_async_copy(staged.at[:, cols], out_ref.at[0, :, cols], out_sem.at[i])
        store.start()
        stores.append(store)
    for tick in (0, 1):
        for child in PARENT:
            for sign in (1, -1):
                gather_copy(tick, PARENT[child], child, sign).wait_send()
                reduce_copy(tick, child, sign).wait_send()
    for copy in swaps + shifts:
        copy.wait_send()
    for store in stores:
        store.wait()


def shards(stream, lengths, routes, norm_gains, router_weights, up_weights, down_weights):
    rows, width = stream.shape[1:]
    own_hidden = up_weights.shape[2]
    experts = router_weights.shape[2]
    main = width // 4 * 3
    sizes = (lax.axis_size("section"), lax.axis_size("expert"), rows, width, own_hidden)
    bf16, f32 = jnp.bfloat16, jnp.float32
    anywhere = pl.BlockSpec(memory_space=pl.ANY)
    vmem = pl.BlockSpec(memory_space=pltpu.VMEM)
    dma = pltpu.SemaphoreType.DMA
    return pl.pallas_call(
        functools.partial(body, sizes),
        out_shape=jax.ShapeDtypeStruct(stream.shape, bf16),
        in_specs=[anywhere, pl.BlockSpec(memory_space=pltpu.SMEM), vmem, vmem, anywhere, anywhere, anywhere],
        out_specs=anywhere,
        scratch_shapes=[
            pltpu.VMEM((rows, width), bf16),
            pltpu.VMEM((rows, width), bf16),
            pltpu.VMEM((rows, width), bf16),
            pltpu.VMEM((rows, rows), bf16),
            pltpu.VMEM((rows, rows), bf16),
            pltpu.VMEM((width, own_hidden), bf16),
            pltpu.VMEM((width, own_hidden), bf16),
            pltpu.VMEM((width, 128), bf16),
            pltpu.VMEM((2 * own_hidden, width), bf16),
            pltpu.VMEM((width, experts), bf16),
            pltpu.VMEM((2, 16, 16, main), bf16),
            pltpu.VMEM((256, width), bf16),
            pltpu.VMEM((256, 2 * own_hidden), bf16),
            pltpu.VMEM((256, width), f32),
            pltpu.VMEM((16, 16, main), f32),
            pltpu.VMEM((2, 2, 9, 16, main), bf16),
            pltpu.VMEM((2, 2, 9, 16, main), bf16),
            pltpu.VMEM((16, main), bf16),
            pltpu.VMEM((16, main), bf16),
            pltpu.VMEM((rows, width), bf16),
            dma((5,)),
            dma((3,)),
            dma((3,)),
            dma((3,)),
            dma((3,)),
            dma((2, 2, 9)),
            dma((2, 2, 9)),
            dma((2, 2, 9)),
            dma((2, 2, 9)),
            dma((4,)),
        ],
        compiler_params=pltpu.CompilerParams(
            collective_id=0, has_side_effects=True, vmem_limit_bytes=48 * 1024 * 1024
        ),
    )(stream, lengths, routes, norm_gains, router_weights, up_weights, down_weights)


def solution(mesh):
    in_specs = (
        P("section", "expert", None),
        P("section", None),
        P(None, "section", "expert", None),
        P("section", None),
        P("section", None, None),
        P("section", None, "expert"),
        P("section", "expert", None),
    )
    out_specs = P("section", "expert", None)
    return jax.shard_map(shards, mesh=mesh, in_specs=in_specs, out_specs=out_specs, check_vma=False)
```

time: 408 us -> 113 us (0.28)
  the two profiles are of different devices: /device:TPU:102 before, /device:TPU:64 now
where the time goes in v1:
time: 113 us
  Pallas kernels  105 us (93%)
  local copies, waits for them, and re-layouts  8.06 us (7%)
    pallas_call x1, Pallas kernels, shards(): pl.pallas_call(functools.partial(body, sizes), out_shape=jax.ShapeDtypeSt...  105 us
    unnamed x12, local copies, waits for them, and re-layouts  8.06 us

profile of v1, /device:TPU:64, one launch (start us, length us, event | category | flops | bytes accessed | tf_op | source)
XLA Modules:
  0.0 113.2 jit_solution(8959914420013763062)
XLA Ops:
  0.0 0.8 copy.8.routes_ref
  0.8 1.3 %copy.9.router_ref = bf16[1,2560,64]{2,1,0:T(8,128)(2,1)S(1)} copy(bf16[1,2560,64]{1,2,0:T(8,128)(2,1)} %param.11) | data formatting | bytes 655360 | tf_op args[4]
  2.1 0.0 copy-start.1
  2.1 0.0 copy-start.2
  2.1 0.0 copy-start.3
  2.2 3.7 %copy.10.up_ref = bf16[1,2560,320]{2,1,0:T(8,128)(2,1)S(1)} copy(bf16[1,2560,320]{1,2,0:T(8,128)(2,1)} %param.12) | data formatting | bytes 3276800 | tf_op args[5]
  5.8 0.0 copy-done.1
  5.8 0.0 copy-done.2
  5.9 0.0 copy-done.3
  5.9 0.0 copy-start
  5.9 1.4 %copy-done = bf16[1,320,2560]{2,1,0:T(8,128)(2,1)S(1)} copy-done((bf16[1,320,2560]{2,1,0:T(8,128)(2,1)S(1)}, bf16[1,320,2560]{2,1,0:T(8,128)(2,1)}, u32[]{:S(2)}) %copy-start) | copy-done | bytes 1638424
  7.3 105.0 %shard_map.73 = bf16[1,128,2560]{2,1,0:T(8,128)(2,1)S(1)} custom-call(bf16[1,128,2560]{2,1,0:T(8,128)(2,1)S(1)} %copy-done.1, s32[1,16]{1,0:T(1,128)S(1)} %copy-done.3, s32[2,1,128,2]{3,2,1,0:T(8,128)S(1)} %copy.8.routes_ref, bf16[1,2560]{1,0:T(2,128)(2,1)S(1)} %copy-done.2, bf16[1,2560,64]{2,1,0:T(8,128)(2,1)S(1)} %copy.9.router_ref, ...), custom_call_target="tpu_custom_call" | custom-call | tf_op jit(solution)/shard_map/pallas_call | solution.py:354
  112.3 0.8 copy.12
Async XLA Ops:
  2.1 3.7 %copy-start.1 = (bf16[1,128,2560]{2,1,0:T(8,128)(2,1)S(1)}, bf16[1,128,2560]{2,1,0:T(8,128)(2,1)}, u32[]{:S(2)}) copy-start(bf16[1,128,2560]{2,1,0:T(8,128)(2,1)} %stream_ref.1) | copy-start | bytes 1966084
  2.1 3.7 %copy-start.2 = (bf16[1,2560]{1,0:T(2,128)(2,1)S(1)}, bf16[1,2560]{1,0:T(2,128)(2,1)}, u32[]{:S(2)}) copy-start(bf16[1,2560]{1,0:T(2,128)(2,1)} %gains_ref.1) | copy-start | bytes 15364
  2.1 3.7 %copy-start.3 = (s32[1,16]{1,0:T(1,128)S(1)}, s32[1,16]{1,0:T(1,128)}, u32[]{:S(2)}) copy-start(s32[1,16]{1,0:T(1,128)} %lengths_ref.1) | copy-start | bytes 196
  5.9 1.4 %copy-start = (bf16[1,320,2560]{2,1,0:T(8,128)(2,1)S(1)}, bf16[1,320,2560]{2,1,0:T(8,128)(2,1)}, u32[]{:S(2)}) copy-start(bf16[1,320,2560]{2,1,0:T(8,128)(2,1)} %down_ref.1) | copy-start | bytes 4915204

commit v2 on v1

v2 whole, which is shorter than its diff:
```python
import functools

import jax
import jax.numpy as jnp
from jax import lax
from jax.experimental import pallas as pl
from jax.experimental.pallas import tpu as pltpu
from jax.sharding import PartitionSpec as P

MESH = pl.DeviceIdType.MESH
EPSILON = 1e-06
CAPACITY = 12
VMEM_LIMIT = 60 * 1024 * 1024

CHILDREN = {0: (3, 1), 3: (6, 4, 2), 6: (8, 7, 5)}
STAGES = (((3,), (1,)), ((6,), (4, 2)), ((), (8, 7, 5)))
PARENT = {child: node for node, kids in CHILDREN.items() for child in kids}
FAR = 8


def slot_order():
    order, groups = [(0, 1)], []
    for inner, leaves in STAGES:
        first = len(order) if groups else 0
        for node in inner + leaves:
            order += [(node, 1)] if node == FAR else [(node, 1), (node, -1)]
        groups.append((first, len(order)))
    places = {pair: place for place, pair in enumerate(order)}
    places[(FAR, -1)] = places[(FAR, 1)]
    places[(0, -1)] = 0
    return places, groups


PLACE, GROUPS = slot_order()
PIECES = 3


def travels(node, sign, piece):
    return node != FAR or (piece < 2) == (sign > 0)


OFFSETS = sorted({sign * (child - node) for child, node in PARENT.items() for sign in (1, -1)})


def body(
    sizes,
    stream_ref, lengths_ref, routes_ref, gains_ref, router_ref, up_ref, down_ref,
    out_ref,
    held, held_prev, merged, info, info_prev, up_all, down_all, router_all,
    gathered, unpacked, hidden, raw, packed_sums, outgoing, incoming, own_sum, own_prev, gate_out, gate_prev, staged,
    local_sem, swap_send, swap_recv, shift_send, shift_recv,
    gather_send, gather_recv, reduce_send, reduce_recv, out_sem,
):
    sections, ranks, rows, width, own_hidden = sizes
    main = width // 4 * 3
    part = main // 3
    mine, theirs = pl.ds(0, own_hidden), pl.ds(own_hidden, own_hidden)
    section = lax.axis_index("section")
    rank = lax.axis_index("expert")
    chip, core = rank // 2, lax.rem(rank, 2)
    sibling = (section, rank + 1 - 2 * core)
    following = (lax.rem(section + 1, sections), rank)
    previous = (lax.rem(section + sections - 1, sections), rank)

    def along(steps):
        return (section, lax.rem(rank + 2 * steps + ranks, ranks))

    def onward(steps):
        return (following[0], lax.rem(rank + 2 * steps + ranks, ranks))

    def backward(steps):
        return (previous[0], lax.rem(rank + 2 * steps + ranks, ranks))

    columns = [pl.ds(i * part, part) for i in range(PIECES)]

    def remote(src, dst, send, recv, device):
        return pltpu.make_async_remote_copy(
            src_ref=src, dst_ref=dst, send_sem=send, recv_sem=recv, device_id=device, device_id_type=MESH
        )

    loads = [
        pltpu.make_async_copy(stream_ref.at[0], held, local_sem.at[0]),
        pltpu.make_async_copy(router_ref.at[0], router_all, local_sem.at[1]),
        pltpu.make_async_copy(up_ref.at[0], up_all.at[mine], local_sem.at[2]),
        pltpu.make_async_copy(down_ref.at[0], down_all.at[mine], local_sem.at[3]),
    ]
    for load in loads:
        load.start()

    barrier = pltpu.get_barrier_semaphore()
    last_hops = sorted({sign * child for child in CHILDREN[0] for sign in (1, -1)}) + [0]
    peers = [along(offset) for offset in OFFSETS] + [sibling]
    peers += [place(offset) for place in (onward, backward) for offset in last_hops]
    for peer in peers:
        pl.semaphore_signal(barrier, inc=1, device_id=peer, device_id_type=MESH)

    lane = lax.broadcasted_iota(jnp.int32, (rows, rows), 1)
    row = lax.broadcasted_iota(jnp.int32, (rows, rows), 0)
    before = (row < lane).astype(jnp.bfloat16)
    slot_row = lax.broadcasted_iota(jnp.int32, (16, part), 0)
    gain = gains_ref[...].astype(jnp.float32)

    def pack(value):
        tail = value[:, main:]
        pieces = []
        for i in range(3):
            moved = pltpu.roll(tail, 12 - 4 * i, 0)
            pieces.append(jnp.where(slot_row < CAPACITY, value[:, i * part : (i + 1) * part], moved))
        return pieces

    def tail_of(pieces):
        result = pltpu.roll(pieces[0], 4, 0)
        result = jnp.where(slot_row < 4, result, pltpu.roll(pieces[1], 8, 0))
        result = jnp.where(slot_row < 8, result, pltpu.roll(pieces[2], 12, 0))
        return result

    def placing(first, second, validity):
        hit = ((first == section) | (second == section)).astype(jnp.float32) * validity
        hit = jnp.broadcast_to(hit, (rows, rows))
        slot = jnp.dot(hit.astype(jnp.bfloat16), before, preferred_element_type=jnp.float32)
        return jnp.where((slot == row.astype(jnp.float32)) & (hit > 0.5), 1.0, 0.0)

    def normalize(x):
        mean_square = jnp.sum(x * x, axis=-1, keepdims=True) * (1.0 / width)
        return x * lax.rsqrt(mean_square + EPSILON) * gain

    def gates(normed, picked, first, second):
        logits = lax.dot_general(
            normed, router_all[...], (((1,), (1,)), ((), ())), preferred_element_type=jnp.float32
        )
        ids = lax.broadcasted_iota(jnp.int32, logits.shape, 1).astype(jnp.float32)
        chosen = [jnp.sum(picked * q.astype(jnp.float32), axis=1, keepdims=True) for q in (first, second)]
        a, b = (jnp.sum(jnp.where(ids == q, logits, 0.0), axis=-1, keepdims=True) for q in chosen)
        first_gate = 1.0 / (1.0 + jnp.exp(b - a))
        second_gate = 1.0 / (1.0 + jnp.exp(a - b))
        window = section.astype(jnp.float32)
        return jnp.where(chosen[0] == window, first_gate, jnp.where(chosen[1] == window, second_gate, 0.0))

    def gather_copy(tick, node, child, sign, piece):
        cols = columns[piece]
        way = 0 if sign > 0 else 1
        return remote(
            gathered.at[tick, PLACE[(node, sign)], :, cols],
            gathered.at[tick, PLACE[(child, sign)], :, cols],
            gather_send.at[tick, way, child, piece],
            gather_recv.at[tick, way, child, piece],
            along(sign * (child - node)),
        )

    def reduce_copy(tick, child, sign, piece):
        cols = columns[piece]
        way = 0 if sign > 0 else 1
        steps = sign * (child - PARENT[child])
        return remote(
            outgoing.at[tick, way, child, :, cols],
            incoming.at[tick, way, child, :, cols],
            reduce_send.at[tick, way, child, piece],
            reduce_recv.at[tick, way, child, piece],
            onward(steps) if tick == 0 and PARENT[child] == 0 else along(steps),
        )

    def both(node):
        return [(piece, sign) for piece in range(PIECES) for sign in (1, -1) if travels(node, sign, piece)]

    def arrive(tick, node, pass_on):
        for piece, sign in both(node):
            gather_copy(tick, PARENT[node], node, sign, piece).wait_recv()
            if pass_on:
                forward(tick, node, piece, sign)

    def forward(tick, node, piece, sign):
        for child in CHILDREN[node]:
            if child in CHILDREN:
                gather_copy(tick, node, child, sign, piece).start()

    def forward_leaves(tick, node):
        for child in CHILDREN[node]:
            if child not in CHILDREN:
                for piece, sign in both(child):
                    gather_copy(tick, node, child, sign, piece).start()

    def expert(tick, first, last):
        low, count = 16 * first, 16 * (last - first)
        for place in range(first, last):
            at = pl.ds(16 * place, 16)
            block = gathered[tick, place]
            unpacked[at, 0:main] = block
            wider = block.astype(jnp.float32)
            tail = tail_of([wider[:, i * part : (i + 1) * part] for i in range(3)])
            unpacked[at, main:width] = tail.astype(jnp.bfloat16)
        at = pl.ds(low, count)
        tokens = unpacked[at, :]
        for begin in range(0, 2 * own_hidden, 256):
            end = min(begin + 256, 2 * own_hidden)
            inner = lax.dot_general(
                tokens, up_all[begin:end, :], (((1,), (1,)), ((), ())), preferred_element_type=jnp.float32
            )
            hidden[at, begin:end] = jax.nn.gelu(inner).astype(jnp.bfloat16)
        active = hidden[at, :]
        for begin in range(0, width, 512):
            raw[at, begin : begin + 512] = jnp.dot(
                active, down_all[:, begin : begin + 512], preferred_element_type=jnp.float32
            )
        for place in range(first, last):
            for i, piece in enumerate(pack(raw[pl.ds(16 * place, 16), :])):
                packed_sums[place, :, i * part : (i + 1) * part] = piece

    def send_sum(tick, node):
        for piece, sign in both(node):
            way = 0 if sign > 0 else 1
            cols = columns[piece]
            total = packed_sums[PLACE[(node, -sign)], :, cols]
            for child in CHILDREN.get(node, ()):
                if travels(child, sign, piece):
                    reduce_copy(tick, child, sign, piece).wait_recv()
                    total = total + incoming[tick, way, child, :, cols].astype(jnp.float32)
            outgoing[tick, way, node, :, cols] = total.astype(jnp.bfloat16)
            reduce_copy(tick, node, sign, piece).start()

    def spread_and_sum(tick, normed, meanwhile, weights_ready=None, first_done=None):
        for i, piece in enumerate(pack(normed)):
            gathered[tick, 0, :, i * part : (i + 1) * part] = piece.astype(jnp.bfloat16)
        for piece, sign in both(0):
            forward(tick, 0, piece, sign)
        forward_leaves(tick, 0)
        meanwhile()
        for (inner, leaves), (first, last) in zip(STAGES, GROUPS):
            for node in inner:
                arrive(tick, node, True)
                forward_leaves(tick, node)
            for node in leaves:
                arrive(tick, node, False)
            if first == 0 and weights_ready:
                weights_ready()
            expert(tick, first, last)
            if first == 0 and first_done:
                first_done()
            for node in leaves:
                send_sum(tick, node)
        for inner, _ in reversed(STAGES):
            for node in inner:
                send_sum(tick, node)

    def summed(tick, own):
        pieces = []
        for piece in range(PIECES):
            total = own[:, piece * part : (piece + 1) * part].astype(jnp.float32)
            for child in CHILDREN[0]:
                for sign in (1, -1):
                    reduce_copy(tick, child, sign, piece).wait_recv()
                    way = 0 if sign > 0 else 1
                    total = total + incoming[tick, way, child, :, columns[piece]].astype(jnp.float32)
            pieces.append(total)
        keep = slot_row < CAPACITY
        whole = [jnp.where(keep, p, 0.0) for p in pieces + [tail_of(pieces)]]
        return jnp.concatenate(whole, axis=1).astype(jnp.bfloat16).astype(jnp.float32)

    own_length = lengths_ref[0, chip]
    position = core * rows + lane[0:1]
    validity = (position < own_length).astype(jnp.float32)
    first, second = routes_ref[0, 0, 0:1], routes_ref[0, 0, 1:2]
    picked = placing(first, second, validity)
    info[...] = jnp.where(row < 16, picked, validity).astype(jnp.bfloat16)
    picked = picked[0:16]
    loads[0].wait()
    x = jnp.dot(picked.astype(jnp.bfloat16), held[...], preferred_element_type=jnp.float32)
    normed = normalize(x).astype(jnp.bfloat16)
    pl.semaphore_wait(barrier, len(peers))

    swaps = [
        remote(up_ref.at[0], up_all.at[theirs], swap_send.at[0], swap_recv.at[0], sibling),
        remote(down_ref.at[0], down_all.at[theirs], swap_send.at[1], swap_recv.at[1], sibling),
    ]
    shifts = [
        remote(info, info_prev, shift_send.at[0], shift_recv.at[0], following),
        remote(stream_ref.at[0], held_prev, shift_send.at[1], shift_recv.at[1], following),
        remote(gate_out, gate_prev, shift_send.at[2], shift_recv.at[2], following),
        remote(own_sum, own_prev, shift_send.at[3], shift_recv.at[3], following),
    ]
    def first_meanwhile():
        for copy in swaps + shifts[:2]:
            copy.start()
        loads[1].wait()
        gate_out[...] = jnp.broadcast_to(gates(normed, picked, first, second), gate_out.shape)
        shifts[2].start()

    def first_done():
        own_sum[...] = packed_sums[0].astype(jnp.bfloat16)
        shifts[3].start()

    def weights_ready():
        for load in loads[2:]:
            load.wait()
        for copy in swaps:
            copy.wait_recv()

    spread_and_sum(0, normed.astype(jnp.float32), first_meanwhile, weights_ready, first_done)

    shifts[0].wait_recv()
    prior = info_prev[...].astype(jnp.float32)
    live = prior[64:65] * (section != 0).astype(jnp.float32)
    prior_picked = jnp.where(row < 16, prior, 0.0)
    prior_spread = jnp.transpose(prior_picked)
    renewed_row = jnp.sum(prior_picked, axis=0, keepdims=True)
    renewed = jnp.sum(prior_spread, axis=1, keepdims=True)
    first2, second2 = routes_ref[1, 0, 0:1], routes_ref[1, 0, 1:2]
    picked2 = placing(first2, second2, live)
    spread2 = jnp.transpose(picked2)
    hit2 = jnp.sum(spread2, axis=1, keepdims=True)
    picked2 = picked2[0:16]
    old_rows = (picked2 * (1.0 - renewed_row)).astype(jnp.bfloat16)
    new_rows = jnp.dot(
        picked2.astype(jnp.bfloat16), prior_spread.astype(jnp.bfloat16), preferred_element_type=jnp.float32
    )
    new_rows = new_rows[:, 0:16].astype(jnp.bfloat16)
    shifts[1].wait_recv()
    kept = jnp.dot(old_rows, held_prev[...], preferred_element_type=jnp.float32)

    prior_x = jnp.dot(prior_picked[0:16].astype(jnp.bfloat16), held_prev[...], preferred_element_type=jnp.float32)
    shifts[2].wait_recv()
    prior_gate = gate_prev[:, 0:1]
    shifts[3].wait_recv()
    update = (prior_x + prior_gate * summed(0, own_prev)).astype(jnp.bfloat16)
    x2 = kept + jnp.dot(new_rows, update, preferred_element_type=jnp.float32)
    normed2 = normalize(x2).astype(jnp.bfloat16)

    gate = []

    def second_meanwhile():
        gate.append(gates(normed2, picked2, first2, second2))
        placed = jnp.dot(
            prior_spread[:, 0:16].astype(jnp.bfloat16), update, preferred_element_type=jnp.float32
        ).astype(jnp.bfloat16)
        merged[...] = jnp.where(renewed > 0.5, placed, held_prev[...])

    spread_and_sum(1, normed2.astype(jnp.float32), second_meanwhile)
    final = (x2 + gate[0] * summed(1, packed_sums.at[0])).astype(jnp.bfloat16)
    spread_final = spread2[:, 0:16].astype(jnp.bfloat16)
    struck = hit2 > 0.5
    stores = []
    for i in range(4):
        cols = pl.ds(i * part, part)
        placed = jnp.dot(spread_final, final[:, i * part : (i + 1) * part], preferred_element_type=jnp.float32)
        staged[:, cols] = jnp.where(struck, placed.astype(jnp.bfloat16), merged[:, cols])
        store = pltpu.make_async_copy(staged.at[:, cols], out_ref.at[0, :, cols], out_sem.at[i])
        store.start()
        stores.append(store)
    for tick in (0, 1):
        for child in PARENT:
            for piece, sign in both(child):
                gather_copy(tick, PARENT[child], child, sign, piece).wait_send()
                reduce_copy(tick, child, sign, piece).wait_send()
    for copy in swaps + shifts:
        copy.wait_send()
    for store in stores:
        store.wait()


def shards(stream, lengths, routes, norm_gains, router_weights, up_weights, down_weights):
    rows, width = stream.shape[1:]
    own_hidden = up_weights.shape[2]
    experts = router_weights.shape[2]
    main = width // 4 * 3
    sizes = (lax.axis_size("section"), lax.axis_size("expert"), rows, width, own_hidden)
    bf16, f32 = jnp.bfloat16, jnp.float32
    anywhere = pl.BlockSpec(memory_space=pl.ANY)
    vmem = pl.BlockSpec(memory_space=pltpu.VMEM)
    dma = pltpu.SemaphoreType.DMA
    return pl.pallas_call(
        functools.partial(body, sizes),
        out_shape=jax.ShapeDtypeStruct(stream.shape, bf16),
        in_specs=[anywhere, pl.BlockSpec(memory_space=pltpu.SMEM), vmem, vmem, anywhere, anywhere, anywhere],
        out_specs=anywhere,
        scratch_shapes=[
            pltpu.VMEM((rows, width), bf16),
            pltpu.VMEM((rows, width), bf16),
            pltpu.VMEM((rows, width), bf16),
            pltpu.VMEM((rows, rows), bf16),
            pltpu.VMEM((rows, rows), bf16),
            pltpu.VMEM((2 * own_hidden, width), bf16),
            pltpu.VMEM((2 * own_hidden, width), bf16),
            pltpu.VMEM((experts, width), bf16),
            pltpu.VMEM((2, 16, 16, main), bf16),
            pltpu.VMEM((256, width), bf16),
            pltpu.VMEM((256, 2 * own_hidden), bf16),
            pltpu.VMEM((256, width), f32),
            pltpu.VMEM((16, 16, main), f32),
            pltpu.VMEM((2, 2, 9, 16, main), bf16),
            pltpu.VMEM((2, 2, 9, 16, main), bf16),
            pltpu.VMEM((16, main), bf16),
            pltpu.VMEM((16, main), bf16),
            pltpu.VMEM((16, 128), f32),
            pltpu.VMEM((16, 128), f32),
            pltpu.VMEM((rows, width), bf16),
            dma((4,)),
            dma((2,)),
            dma((2,)),
            dma((4,)),
            dma((4,)),
            dma((2, 2, 9, PIECES)),
            dma((2, 2, 9, PIECES)),
            dma((2, 2, 9, PIECES)),
            dma((2, 2, 9, PIECES)),
            dma((4,)),
        ],
        compiler_params=pltpu.CompilerParams(
            collective_id=0, has_side_effects=True, vmem_limit_bytes=VMEM_LIMIT
        ),
    )(
        stream,
        lengths,
        jnp.swapaxes(routes, 2, 3),
        norm_gains,
        jnp.swapaxes(router_weights, 1, 2),
        jnp.swapaxes(up_weights, 1, 2),
        down_weights,
    )


def solution(mesh):
    in_specs = (
        P("section", "expert", None),
        P("section", None),
        P(None, "section", "expert", None),
        P("section", None),
        P("section", None, None),
        P("section", None, "expert"),
        P("section", "expert", None),
    )
    out_specs = P("section", "expert", None)
    return jax.shard_map(shards, mesh=mesh, in_specs=in_specs, out_specs=out_specs, check_vma=False)
```

time: 113 us -> 102 us (0.903)
  the two profiles are of different devices: /device:TPU:64 before, /device:TPU:8 now
where the time goes in v2:
time: 102 us
  Pallas kernels  99.6 us (98%)
  local copies, waits for them, and re-layouts  1.97 us (2%)
    pallas_call x1, Pallas kernels, shards(): pl.pallas_call(functools.partial(body, sizes), out_shape=jax.ShapeDtypeSt...  99.6 us

profile of v2, /device:TPU:8, one launch (start us, length us, event | category | flops | bytes accessed | tf_op | source)
XLA Modules:
  0.0 101.5 jit_solution(8511003801935064068)
XLA Ops:
  0.0 99.6 %shard_map.73 = bf16[1,128,2560]{2,1,0:T(8,128)(2,1)} custom-call(bf16[1,128,2560]{2,1,0:T(8,128)(2,1)} %stream_ref.1, s32[1,16]{1,0:T(1,128)} %lengths_ref.1, s32[2,1,2,128]{3,2,1,0:T(2,128)} %bitcast.5, bf16[1,2560]{1,0:T(2,128)(2,1)} %gains_ref.1, bf16[1,64,2560]{2,1,0:T(8,128)(2,1)} %bitcast.4, bf16[1,320,2560]{2,1,0:T(8,128)(2,1)} %bitcast.3, ...), custom_call_target="tpu_custom_call" | custom-call | tf_op jit(solution)/shard_map/pallas_call | solution.py:369
  99.6 2.0 %copy.9 = bf16[1,128,2560]{2,1,0:T(8,128)(2,1)} copy(bf16[1,128,2560]{2,1,0:T(8,128)(2,1)} %shard_map.73) | data formatting | bytes 1310720

commit v3 on v2

--- a/solution.py
+++ b/solution.py
@@ -16,6 +16,7 @@
 STAGES = (((3,), (1,)), ((6,), (4, 2)), ((), (8, 7, 5)))
 PARENT = {child: node for node, kids in CHILDREN.items() for child in kids}
 FAR = 8
+EAGER = (6,)
 
 
 def slot_order():
@@ -59,17 +60,18 @@
     rank = lax.axis_index("expert")
     chip, core = rank // 2, lax.rem(rank, 2)
     sibling = (section, rank + 1 - 2 * core)
+    forth = 2 - 4 * core
     following = (lax.rem(section + 1, sections), rank)
     previous = (lax.rem(section + sections - 1, sections), rank)
 
     def along(steps):
-        return (section, lax.rem(rank + 2 * steps + ranks, ranks))
+        return (section, lax.rem(rank + forth * steps + ranks, ranks))
 
     def onward(steps):
-        return (following[0], lax.rem(rank + 2 * steps + ranks, ranks))
+        return (following[0], lax.rem(rank + forth * steps + ranks, ranks))
 
     def backward(steps):
-        return (previous[0], lax.rem(rank + 2 * steps + ranks, ranks))
+        return (previous[0], lax.rem(rank + forth * steps + ranks, ranks))
 
     columns = [pl.ds(i * part, part) for i in range(PIECES)]
 
@@ -97,22 +99,29 @@
     lane = lax.broadcasted_iota(jnp.int32, (rows, rows), 1)
     row = lax.broadcasted_iota(jnp.int32, (rows, rows), 0)
     before = (row < lane).astype(jnp.bfloat16)
-    slot_row = lax.broadcasted_iota(jnp.int32, (16, part), 0)
+    low_row = lax.broadcasted_iota(jnp.int32, (8, part), 0)
     gain = gains_ref[...].astype(jnp.float32)
 
+    def pack_upper(value):
+        quarters = [value[:, i * part : (i + 1) * part] for i in range(4)]
+        return [jnp.concatenate(quarters[0:2], axis=0), jnp.concatenate(quarters[2:4], axis=0)]
+
+    def pack_lower(value):
+        quarters = [value[:, i * part : (i + 1) * part] for i in range(4)]
+        halves = [
+            jnp.where(low_row < 4, quarters[i], pltpu.roll(quarters[i + 1], 4, 0)) for i in (0, 2)
+        ]
+        return jnp.concatenate(halves, axis=0)
+
     def pack(value):
-        tail = value[:, main:]
-        pieces = []
-        for i in range(3):
-            moved = pltpu.roll(tail, 12 - 4 * i, 0)
-            pieces.append(jnp.where(slot_row < CAPACITY, value[:, i * part : (i + 1) * part], moved))
-        return pieces
-
-    def tail_of(pieces):
-        result = pltpu.roll(pieces[0], 4, 0)
-        result = jnp.where(slot_row < 4, result, pltpu.roll(pieces[1], 8, 0))
-        result = jnp.where(slot_row < 8, result, pltpu.roll(pieces[2], 12, 0))
-        return result
+        return pack_upper(value[0:8]) + [pack_lower(value[8:16])]
+
+    def upper_of(pieces):
+        return jnp.concatenate([half for p in pieces for half in (p[0:8], p[8:16])], axis=1)
+
+    def lower_of(piece):
+        low, high = piece[0:8], piece[8:16]
+        return jnp.concatenate([low, pltpu.roll(low, 4, 0), high, pltpu.roll(high, 4, 0)], axis=1)
 
     def placing(first, second, validity):
         hit = ((first == section) | (second == section)).astype(jnp.float32) * validity
@@ -159,54 +168,62 @@
             onward(steps) if tick == 0 and PARENT[child] == 0 else along(steps),
         )
 
-    def both(node):
-        return [(piece, sign) for piece in range(PIECES) for sign in (1, -1) if travels(node, sign, piece)]
-
-    def arrive(tick, node, pass_on):
-        for piece, sign in both(node):
+    def both(node, pieces=range(PIECES)):
+        return [(piece, sign) for piece in pieces for sign in (1, -1) if travels(node, sign, piece)]
+
+    def arrive(tick, node, pass_on, pieces=range(PIECES)):
+        for piece, sign in both(node, pieces):
             gather_copy(tick, PARENT[node], node, sign, piece).wait_recv()
             if pass_on:
                 forward(tick, node, piece, sign)
 
     def forward(tick, node, piece, sign):
         for child in CHILDREN[node]:
-            if child in CHILDREN:
+            if (child in CHILDREN or node in EAGER) and travels(child, sign, piece):
                 gather_copy(tick, node, child, sign, piece).start()
 
     def forward_leaves(tick, node):
         for child in CHILDREN[node]:
-            if child not in CHILDREN:
+            if child not in CHILDREN and node not in EAGER:
                 for piece, sign in both(child):
                     gather_copy(tick, node, child, sign, piece).start()
 
-    def expert(tick, first, last):
-        low, count = 16 * first, 16 * (last - first)
-        for place in range(first, last):
-            at = pl.ds(16 * place, 16)
-            block = gathered[tick, place]
-            unpacked[at, 0:main] = block
-            wider = block.astype(jnp.float32)
-            tail = tail_of([wider[:, i * part : (i + 1) * part] for i in range(3)])
-            unpacked[at, main:width] = tail.astype(jnp.bfloat16)
-        at = pl.ds(low, count)
-        tokens = unpacked[at, :]
+    def expert(tick, places, parts):
+        chunks = [(place, upper) for place in places for upper in parts]
+        values = []
+        for place, upper in chunks:
+            if upper:
+                block = gathered[tick, place, :, 0 : 2 * part].astype(jnp.float32)
+                values.append(upper_of([block[:, 0:part], block[:, part:]]))
+            else:
+                values.append(lower_of(gathered[tick, place, :, 2 * part :].astype(jnp.float32)))
+        if len(values) % 2:
+            values.append(values[-1])
+        count = 8 * len(values)
+        for i in range(0, len(values), 2):
+            unpacked[8 * i : 8 * i + 16, :] = jnp.concatenate(values[i : i + 2], axis=0).astype(jnp.bfloat16)
+        tokens = unpacked[0:count, :]
         for begin in range(0, 2 * own_hidden, 256):
             end = min(begin + 256, 2 * own_hidden)
             inner = lax.dot_general(
                 tokens, up_all[begin:end, :], (((1,), (1,)), ((), ())), preferred_element_type=jnp.float32
             )
-            hidden[at, begin:end] = jax.nn.gelu(inner).astype(jnp.bfloat16)
-        active = hidden[at, :]
+            hidden[0:count, begin:end] = jax.nn.gelu(inner).astype(jnp.bfloat16)
+        active = hidden[0:count, :]
         for begin in range(0, width, 512):
-            raw[at, begin : begin + 512] = jnp.dot(
+            raw[0:count, begin : begin + 512] = jnp.dot(
                 active, down_all[:, begin : begin + 512], preferred_element_type=jnp.float32
             )
-        for place in range(first, last):
-            for i, piece in enumerate(pack(raw[pl.ds(16 * place, 16), :])):
-                packed_sums[place, :, i * part : (i + 1) * part] = piece
-
-    def send_sum(tick, node):
-        for piece, sign in both(node):
+        for i, (place, upper) in enumerate(chunks):
+            rows_out = raw[8 * i : 8 * i + 8, :]
+            if upper:
+                for k, piece in enumerate(pack_upper(rows_out)):
+                    packed_sums[place, :, k * part : (k + 1) * part] = piece
+            else:
+                packed_sums[place, :, 2 * part :] = pack_lower(rows_out)
+
+    def send_sum(tick, node, pieces=range(PIECES)):
+        for piece, sign in both(node, pieces):
             way = 0 if sign > 0 else 1
             cols = columns[piece]
             total = packed_sums[PLACE[(node, -sign)], :, cols]
@@ -224,19 +241,35 @@
             forward(tick, 0, piece, sign)
         forward_leaves(tick, 0)
         meanwhile()
+        def work(first, last, leaves):
+            expert(tick, range(first, last), (True, False))
+            if first == 0 and first_done:
+                first_done()
+            for node in leaves:
+                send_sum(tick, node)
+
+        late = []
         for (inner, leaves), (first, last) in zip(STAGES, GROUPS):
             for node in inner:
                 arrive(tick, node, True)
                 forward_leaves(tick, node)
-            for node in leaves:
-                arrive(tick, node, False)
-            if first == 0 and weights_ready:
+            if late:
                 weights_ready()
-            expert(tick, first, last)
-            if first == 0 and first_done:
-                first_done()
-            for node in leaves:
-                send_sum(tick, node)
+                work(*late.pop())
+            if inner:
+                for node in leaves:
+                    arrive(tick, node, False)
+                if first == 0 and weights_ready:
+                    late.append((first, last, leaves))
+                else:
+                    work(first, last, leaves)
+            else:
+                for pieces, upper in (((0, 1), True), ((2,), False)):
+                    for node in leaves:
+                        arrive(tick, node, False, pieces)
+                    expert(tick, range(first, last), (upper,))
+                    for node in leaves:
+                        send_sum(tick, node, pieces)
         for inner, _ in reversed(STAGES):
             for node in inner:
                 send_sum(tick, node)
@@ -251,9 +284,10 @@
                     way = 0 if sign > 0 else 1
                     total = total + incoming[tick, way, child, :, columns[piece]].astype(jnp.float32)
             pieces.append(total)
-        keep = slot_row < CAPACITY
-        whole = [jnp.where(keep, p, 0.0) for p in pieces + [tail_of(pieces)]]
-        return jnp.concatenate(whole, axis=1).astype(jnp.bfloat16).astype(jnp.float32)
+        lower = lower_of(pieces[2])
+        keep = lax.broadcasted_iota(jnp.int32, lower.shape, 0) < CAPACITY - 8
+        whole = jnp.concatenate([upper_of(pieces[0:2]), jnp.where(keep, lower, 0.0)], axis=0)
+        return whole.astype(jnp.bfloat16).astype(jnp.float32)
 
     own_length = lengths_ref[0, chip]
     position = core * rows + lane[0:1]
@@ -278,13 +312,14 @@
         remote(own_sum, own_prev, shift_send.at[3], shift_recv.at[3], following),
     ]
     def first_meanwhile():
-        for copy in swaps + shifts[:2]:
+        for copy in swaps + shifts[:1]:
             copy.start()
         loads[1].wait()
         gate_out[...] = jnp.broadcast_to(gates(normed, picked, first, second), gate_out.shape)
         shifts[2].start()
 
     def first_done():
+        shifts[1].start()
         own_sum[...] = packed_sums[0].astype(jnp.bfloat16)
         shifts[3].start()
 
@@ -381,9 +416,9 @@
             pltpu.VMEM((2 * own_hidden, width), bf16),
             pltpu.VMEM((experts, width), bf16),
             pltpu.VMEM((2, 16, 16, main), bf16),
-            pltpu.VMEM((256, width), bf16),
-            pltpu.VMEM((256, 2 * own_hidden), bf16),
-            pltpu.VMEM((256, width), f32),
+            pltpu.VMEM((128, width), bf16),
+            pltpu.VMEM((128, 2 * own_hidden), bf16),
+            pltpu.VMEM((128, width), f32),
             pltpu.VMEM((16, 16, main), f32),
             pltpu.VMEM((2, 2, 9, 16, main), bf16),
             pltpu.VMEM((2, 2, 9, 16, main), bf16),

time: 102 us -> 96.8 us (0.949)
  the two profiles are of different devices: /device:TPU:8 before, /device:TPU:64 now
where the time goes in v3:
time: 96.8 us; the launch traced here: 96.6 us
  Pallas kernels  94.6 us (98%)
  local copies, waits for them, and re-layouts  1.97 us (2%)
    pallas_call x1, Pallas kernels, shards(): pl.pallas_call(functools.partial(body, sizes), out_shape=jax.ShapeDtypeSt...  94.6 us
    unnamed x1, local copies, waits for them, and re-layouts  1.97 us

profile of v3, /device:TPU:64, one launch (start us, length us, event | category | flops | bytes accessed | tf_op | source)
XLA Modules:
  0.0 96.6 jit_solution(7794090105503592449)
XLA Ops:
  0.0 94.6 %shard_map.73 = bf16[1,128,2560]{2,1,0:T(8,128)(2,1)} custom-call(bf16[1,128,2560]{2,1,0:T(8,128)(2,1)} %stream_ref.1, s32[1,16]{1,0:T(1,128)} %lengths_ref.1, s32[2,1,2,128]{3,2,1,0:T(2,128)} %bitcast.5, bf16[1,2560]{1,0:T(2,128)(2,1)} %gains_ref.1, bf16[1,64,2560]{2,1,0:T(8,128)(2,1)} %bitcast.4, bf16[1,320,2560]{2,1,0:T(8,128)(2,1)} %bitcast.3, ...), custom_call_target="tpu_custom_call" | custom-call | tf_op jit(solution)/shard_map/pallas_call | solution.py:404
  94.7 2.0 %copy.9 = bf16[1,128,2560]{2,1,0:T(8,128)(2,1)} copy(bf16[1,128,2560]{2,1,0:T(8,128)(2,1)} %shard_map.73) | data formatting | bytes 1310720

commit v4 on v3

--- a/solution.py
+++ b/solution.py
@@ -254,12 +254,13 @@
                 arrive(tick, node, True)
                 forward_leaves(tick, node)
             if late:
-                weights_ready()
+                if weights_ready:
+                    weights_ready()
                 work(*late.pop())
             if inner:
                 for node in leaves:
                     arrive(tick, node, False)
-                if first == 0 and weights_ready:
+                if first == 0:
                     late.append((first, last, leaves))
                 else:
                     work(first, last, leaves)

time: 96.8 us -> 97.1 us (level)
  the two profiles are of different devices: /device:TPU:64 before, /device:TPU:8 now
where the time goes in v4:
time: 97.1 us; the launch traced here: 96.9 us
  Pallas kernels  94.9 us (98%)
  local copies, waits for them, and re-layouts  1.97 us (2%)
    pallas_call x1, Pallas kernels, shards(): pl.pallas_call(functools.partial(body, sizes), out_shape=jax.ShapeDtypeSt...  94.9 us
    unnamed x1, local copies, waits for them, and re-layouts  1.97 us

profile of v4, /device:TPU:8, one launch (start us, length us, event | category | flops | bytes accessed | tf_op | source)
XLA Modules:
  0.0 96.9 jit_solution(17042276127946380075)
XLA Ops:
  0.0 94.9 %shard_map.73 = bf16[1,128,2560]{2,1,0:T(8,128)(2,1)} custom-call(bf16[1,128,2560]{2,1,0:T(8,128)(2,1)} %stream_ref.1, s32[1,16]{1,0:T(1,128)} %lengths_ref.1, s32[2,1,2,128]{3,2,1,0:T(2,128)} %bitcast.5, bf16[1,2560]{1,0:T(2,128)(2,1)} %gains_ref.1, bf16[1,64,2560]{2,1,0:T(8,128)(2,1)} %bitcast.4, bf16[1,320,2560]{2,1,0:T(8,128)(2,1)} %bitcast.3, ...), custom_call_target="tpu_custom_call" | custom-call | tf_op jit(solution)/shard_map/pallas_call | solution.py:405
  94.9 2.0 %copy.9 = bf16[1,128,2560]{2,1,0:T(8,128)(2,1)} copy(bf16[1,128,2560]{2,1,0:T(8,128)(2,1)} %shard_map.73) | data formatting | bytes 1310720

commit v5 on v4

--- a/solution.py
+++ b/solution.py
@@ -33,11 +33,11 @@
 
 
 PLACE, GROUPS = slot_order()
-PIECES = 3
+PIECES = 2
 
 
 def travels(node, sign, piece):
-    return node != FAR or (piece < 2) == (sign > 0)
+    return node != FAR or (piece < 1) == (sign > 0)
 
 
 OFFSETS = sorted({sign * (child - node) for child, node in PARENT.items() for sign in (1, -1)})
@@ -73,7 +73,8 @@
     def backward(steps):
         return (previous[0], lax.rem(rank + forth * steps + ranks, ranks))
 
-    columns = [pl.ds(i * part, part) for i in range(PIECES)]
+    spans = ((0, 2 * part), (2 * part, main))
+    columns = [pl.ds(begin, end - begin) for begin, end in spans]
 
     def remote(src, dst, send, recv, device):
         return pltpu.make_async_remote_copy(
@@ -265,7 +266,7 @@
                 else:
                     work(first, last, leaves)
             else:
-                for pieces, upper in (((0, 1), True), ((2,), False)):
+                for pieces, upper in (((0,), True), ((1,), False)):
                     for node in leaves:
                         arrive(tick, node, False, pieces)
                     expert(tick, range(first, last), (upper,))
@@ -278,16 +279,16 @@
     def summed(tick, own):
         pieces = []
         for piece in range(PIECES):
-            total = own[:, piece * part : (piece + 1) * part].astype(jnp.float32)
+            total = own[:, spans[piece][0] : spans[piece][1]].astype(jnp.float32)
             for child in CHILDREN[0]:
                 for sign in (1, -1):
                     reduce_copy(tick, child, sign, piece).wait_recv()
                     way = 0 if sign > 0 else 1
                     total = total + incoming[tick, way, child, :, columns[piece]].astype(jnp.float32)
             pieces.append(total)
-        lower = lower_of(pieces[2])
+        lower = lower_of(pieces[1])
         keep = lax.broadcasted_iota(jnp.int32, lower.shape, 0) < CAPACITY - 8
-        whole = jnp.concatenate([upper_of(pieces[0:2]), jnp.where(keep, lower, 0.0)], axis=0)
+        whole = jnp.concatenate([upper_of([pieces[0][:, 0:part], pieces[0][:, part:]]), jnp.where(keep, lower, 0.0)], axis=0)
         return whole.astype(jnp.bfloat16).astype(jnp.float32)
 
     own_length = lengths_ref[0, chip]

time: 97.1 us -> 98.2 us (1.011)
  Pallas kernels: 94.9 us -> 96 us
    pallas_call x1, Pallas kernels: 94.9 us -> 96 us  [shards(): pl.pallas_call(functools.partial(body, sizes), out_shape=jax.ShapeDtypeSt...]
where the time goes in v5:
time: 98.2 us; the launch traced here: 98 us
  Pallas kernels  96 us (98%)
  local copies, waits for them, and re-layouts  1.97 us (2%)
    pallas_call x1, Pallas kernels, shards(): pl.pallas_call(functools.partial(body, sizes), out_shape=jax.ShapeDtypeSt...  96 us
    unnamed x1, local copies, waits for them, and re-layouts  1.97 us

profile of v5, /device:TPU:8, one launch (start us, length us, event | category | flops | bytes accessed | tf_op | source)
XLA Modules:
  0.0 98.0 jit_solution(8273430838307003612)
XLA Ops:
  0.0 96.0 %shard_map.73 = bf16[1,128,2560]{2,1,0:T(8,128)(2,1)} custom-call(bf16[1,128,2560]{2,1,0:T(8,128)(2,1)} %stream_ref.1, s32[1,16]{1,0:T(1,128)} %lengths_ref.1, s32[2,1,2,128]{3,2,1,0:T(2,128)} %bitcast.5, bf16[1,2560]{1,0:T(2,128)(2,1)} %gains_ref.1, bf16[1,64,2560]{2,1,0:T(8,128)(2,1)} %bitcast.4, bf16[1,320,2560]{2,1,0:T(8,128)(2,1)} %bitcast.3, ...), custom_call_target="tpu_custom_call" | custom-call | tf_op jit(solution)/shard_map/pallas_call | solution.py:406
  96.0 2.0 %copy.9 = bf16[1,128,2560]{2,1,0:T(8,128)(2,1)} copy(bf16[1,128,2560]{2,1,0:T(8,128)(2,1)} %shard_map.73) | data formatting | bytes 1310720
